TPU v7x, 32 devices: a whole 2x2x4 slice. The times are simulated.
32 devices in a mesh: grp: 2 (over y), hid: 4 (over z), feat: 4 (over x, core).
Axes of the slice: x: 2, y: 2, z: 4, core: 2. Of those that a mesh axis runs over, the one named last changes fastest.
Arguments:
- tokens: bfloat16 [128, 8192], P(('grp', 'hid'), 'feat'), parts along dimension 0, may hold values from -6 to 6
- gate_weight: bfloat16 [8192, 16384], P('feat', 'hid'), may hold values from -0.0625 to 0.0625
- up_weight: bfloat16 [8192, 16384], P('feat', 'hid'), may hold values from -0.0625 to 0.0625
- down_weight: bfloat16 [16384, 8192], P('hid', 'feat'), may hold values from -0.046875 to 0.046875
Outputs:
- mixed: bfloat16 [128, 8192], P(('grp', 'hid'), 'feat'), parts along dimension 0
There are 2 independent parts, one for each index of `grp`. A program takes and returns all parts, laid end to end along the dimension named above; an argument that names none is the same for every part. Nothing has to cross between parts.
All inputs are finite; a program needn't handle non-finite values.
Results may differ from a plain program's by a relative error of at most 0.02.
Values may be sent and summed in bfloat16 or wider, within the bound.
A program may use at most 128 MiB of HBM per device.

v0:
```python
import jax
import jax.numpy as jnp
from jax import lax
from jax.sharding import PartitionSpec as P


def swiglu(gate_up, split_at):
    return (jax.nn.silu(gate_up[:, :split_at]) * gate_up[:, split_at:]).astype(jnp.bfloat16)


def shards(tokens, gate_weight, up_weight, down_weight):
    gathered = lax.all_gather(tokens, "hid", axis=0, tiled=True)
    hid_cols = gate_weight.shape[1]
    row_block = gathered
    gate_part = jnp.dot(row_block, gate_weight, preferred_element_type=jnp.float32)
    up_part = jnp.dot(row_block, up_weight, preferred_element_type=jnp.float32)
    gate_up = lax.psum_scatter(
        jnp.concatenate([gate_part, up_part], axis=1).astype(jnp.bfloat16),
        "feat",
        scatter_dimension=0,
        tiled=True,
    ).astype(jnp.float32)
    hidden_share = swiglu(gate_up, hid_cols)
    hidden = lax.all_gather(hidden_share, "feat", axis=0, tiled=True)
    row_block = hidden
    return lax.psum_scatter(
        jnp.dot(row_block, down_weight, preferred_element_type=jnp.float32).astype(jnp.bfloat16),
        "hid",
        scatter_dimension=0,
        tiled=True,
    )


def solution(mesh):
    placed = (P(("grp", "hid"), "feat"), P("feat", "hid"), P("feat", "hid"), P("hid", "feat"))
    return jax.shard_map(
        shards, mesh=mesh, in_specs=placed, out_specs=P(("grp", "hid"), "feat"), check_vma=False
    )
```

profile of v0, /device:TPU:0, one launch (start us, length us, event | category | flops | bytes accessed | tf_op | source)
XLA Modules:
  0.0 106.4 jit_solution(1129384321267286692)
XLA Ops:
  6.5 0.0 reduce-scatter.3.cloned.1.call-start
  6.5 0.0 copy-start
  6.5 16.0 %all_gather.6 = bf16[64,2048]{1,0:T(8,128)(2,1)S(1)} all-gather(bf16[16,2048]{1,0:T(8,128)(2,1)} %param.4), channel_id=1, replica_groups=mesh['grp'=2,'hid'=4,'feat'=4] {'hid'}, dimensions={0}, use_global_device_ids=true | all-gather | bytes 327680 | tf_op jit(solution)/shard_map/all_gather | solution.py:12
  22.5 8.8 %convolution_convert_fusion = bf16[64,4096]{1,0:T(8,128)(2,1)S(1)} fusion(bf16[64,2048]{1,0:T(8,128)(2,1)S(1)} %all_gather.6, bf16[2048,4096]{1,0:T(8,128)(2,1)} %param.6), kind=kOutput, calls=%fused_computation | convolution fusion | flops 1074003968 | bytes 17563648 | tf_op jit(solution)/shard_map/dot_general | solution.py:16
  31.3 0.0 copy-done
  31.3 3.0 %convolution_convert_fusion.1 = bf16[64,4096]{1,0:T(8,128)(2,1)S(1)} fusion(bf16[64,2048]{1,0:T(8,128)(2,1)S(1)} %all_gather.6, bf16[2048,4096]{1,0:T(8,128)(2,1)S(1)} %copy-done), kind=kOutput, calls=%fused_computation.1 | convolution fusion | flops 1074003968 | bytes 17563648 | tf_op jit(solution)/shard_map/dot_general | solution.py:15
  34.4 1.0 pad_maximum_fusion
  35.4 0.0 reduce-scatter.3.cloned.1.call-update
  35.4 0.0 reduce-scatter.5.cloned.1.call-start
  35.5 26.5 %reduce-scatter.3.cloned.1.call-done = bf16[16,8192]{1,0:T(8,128)(2,1)} async-done(((bf16[64,8192]{1,0:T(8,128)(2,1)}), bf16[16,8192]{1,0:T(8,128)(2,1)}) %reduce-scatter.3.cloned.1.call-update) | async-done | bytes 262160 | tf_op jit(solution)/shard_map/reduce_scatter | solution.py:17
  62.0 1.0 convert_element_type.10
  63.0 0.1 fusion
  63.1 6.8 %all_gather.7 = bf16[64,4096]{1,0:T(8,128)(2,1)S(1)} all-gather(bf16[16,4096]{1,0:T(8,128)(2,1)S(1)} %fusion), channel_id=1, replica_groups=mesh['grp'=2,'hid'=4,'feat'=4] {'feat'}, dimensions={0}, use_global_device_ids=true | all-gather | bytes 655360 | tf_op jit(solution)/shard_map/all_gather | solution.py:24
  69.9 9.5 %convolution_convert_fusion.2 = bf16[64,2048]{1,0:T(8,128)(2,1)} fusion(bf16[64,4096]{1,0:T(8,128)(2,1)S(1)} %all_gather.7, bf16[4096,2048]{1,0:T(8,128)(2,1)} %param.7), kind=kOutput, calls=%fused_computation.2 | convolution fusion | flops 1073872896 | bytes 17563648 | tf_op jit(solution)/shard_map/dot_general | solution.py:27
  79.4 0.0 reduce-scatter.5.cloned.1.call-update
  79.4 20.2 %reduce-scatter.5.cloned.1.call-done = bf16[16,2048]{1,0:T(8,128)(2,1)} async-done(((bf16[64,2048]{1,0:T(8,128)(2,1)}), bf16[16,2048]{1,0:T(8,128)(2,1)}) %reduce-scatter.5.cloned.1.call-update) | async-done | bytes 65552 | tf_op jit(solution)/shard_map/reduce_scatter | solution.py:26
Async XLA Ops:
  6.5 55.5 %reduce-scatter.3.cloned.1.call-start = ((), (), s32[]{:S(2)}) async-start(), calls=%async_computation.2 | async-start | bytes 1310720 | tf_op jit(solution)/shard_map/reduce_scatter | solution.py:17
  6.5 24.8 %copy-start = (bf16[2048,4096]{1,0:T(8,128)(2,1)S(1)}, bf16[2048,4096]{1,0:T(8,128)(2,1)}, u32[]{:S(2)}) copy-start(bf16[2048,4096]{1,0:T(8,128)(2,1)} %param.5) | copy-start | bytes 50331652
  35.4 64.1 %reduce-scatter.5.cloned.1.call-start = ((), (), s32[]{:S(2)}) async-start(), calls=%async_computation.3 | async-start | bytes 327680 | tf_op jit(solution)/shard_map/reduce_scatter | solution.py:26
Sparse Core Ops, SparseCore 0:
  35.6 26.4 reduce-scatter.2
  79.5 20.0 reduce-scatter.4
where the time goes:
time: 107 us; the launch traced here: 106 us
  waiting for transfers between devices  46.8 us (44%)
  blocking collectives  22.7 us (21%)
  matrix products  21.3 us (20%)
  between operations  13.4 us (13%)
  other arithmetic  2.11 us (2%)
    reduce_scatter x1, waiting for transfers between devices, shards(): lax.psum_scatter(jnp.concatenate([gate_part, up_part], axis=1).astype(jnp...  26.5 us
    reduce_scatter x1, waiting for transfers between devices, shards(): lax.psum_scatter(jnp.dot(row_block, down_weight, preferred_element_type=j...  20.2 us
    all_gather x1, blocking collectives, shards(): gathered = lax.all_gather(tokens, 'hid', axis=0, tiled=True)  16 us
    dot_general x1, matrix products, shards(): jnp.dot(row_block, down_weight, preferred_element_type=jnp.float32)  9.49 us
    dot_general x1, matrix products, shards(): up_part = jnp.dot(row_block, up_weight, preferred_element_type=jnp.float32)  8.8 us
    all_gather x1, blocking collectives, shards(): hidden = lax.all_gather(hidden_share, 'feat', axis=0, tiled=True)  6.76 us
    dot_general x1, matrix products, shards(): jnp.dot(row_block, gate_weight, preferred_element_type=jnp.float32)  3.04 us
  transfers between devices with their start and end apart: 2, of which 2 were waited for; matrix products, arithmetic and copies ran while one was open for 0% of the time, Pallas kernels for 0%

commit v1 on v0

v1 whole, which is shorter than its diff:
```python
import functools

import jax
import jax.numpy as jnp
from jax import lax
from jax.experimental import pallas as pl
from jax.experimental.pallas import tpu as pltpu
from jax.sharding import PartitionSpec as P

MESH = pl.DeviceIdType.MESH
F32, BF16 = jnp.float32, jnp.bfloat16


def each(count, body):
    if count <= 4:
        for i in range(count):
            body(i)
    else:
        lax.fori_loop(0, count, lambda i, _: (body(i), 0)[1], 0)


def kernel(
    H, X, tok_ref, gate_ref, up_ref, down_ref, out_ref,
    tok, wg, wu, wd, part, pair_in, x_out, x_in, hid, o_part, o_in,
    wg_sem, wu_sem, wd_sem, own_sem, tok_s, tok_r, pair_s, pair_r, x_s, x_r,
    hp_s, hp_r, hx_s, hx_r, hf_s, hf_r, o_s, o_r,
):
    nch, _, cn = wg.shape
    nd, _, dn = wd.shape
    F = 2 * X
    rf = part.shape[3]
    r_in = tok.shape[1]
    rows = H * r_in
    ob = max(2, min(F, 256 // rf))
    block = ob * rf

    h = lax.axis_index("hid")
    f = lax.axis_index("feat")
    x, c = lax.div(f, 2), lax.rem(f, 2)
    pair = {"feat": x * 2 + 1 - c}

    def x_peer(d):
        return lax.rem(x + d, X)

    def remote(src, dst, ssem, rsem, device):
        return pltpu.make_async_remote_copy(
            src_ref=src, dst_ref=dst, send_sem=ssem, recv_sem=rsem,
            device_id=device, device_id_type=MESH,
        )

    def cols(ref, k, n):
        return ref.at[:, pl.ds(pl.multiple_of(k * n, n), n)]

    def wg_copy(k):
        return pltpu.make_async_copy(cols(gate_ref, k, cn), wg.at[k], wg_sem.at[k])

    def wu_copy(k):
        return pltpu.make_async_copy(cols(up_ref, k, cn), wu.at[k], wu_sem.at[k])

    def wd_copy(n):
        return pltpu.make_async_copy(cols(down_ref, n, dn), wd.at[n], wd_sem.at[n])

    def tok_copy(d):
        to = lax.rem(h + d + 1, H)
        return remote(tok_ref, tok.at[h], tok_s.at[d], tok_r.at[d], {"hid": to})

    def pair_copy(k):
        return remote(part.at[k, :, 1 - c], pair_in.at[k], pair_s.at[k], pair_r.at[k], pair)

    def x_copy(k, d):
        to = {"feat": x_peer(d + 1) * 2 + c}
        return remote(x_out.at[k, d], x_in.at[k, d], x_s.at[k, d], x_r.at[k, d], to)

    def hp_copy(k):
        return remote(hid.at[k, f], hid.at[k, f], hp_s.at[k], hp_r.at[k], pair)

    def hx_copy(k, d):
        to = {"feat": x_peer(d + 1) * 2 + c}
        return remote(hid.at[k, f], hid.at[k, f], hx_s.at[k, d], hx_r.at[k, d], to)

    def hf_copy(k, d):
        owner = lax.rem(x + X - d - 1, X) * 2 + c
        piece = hid.at[k, owner]
        return remote(piece, piece, hf_s.at[k, d], hf_r.at[k, d], pair)

    def o_copy(n, d):
        to = lax.rem(h + d + 1, H)
        return remote(o_part.at[n, to], o_in.at[n, d], o_s.at[n, d], o_r.at[n, d], {"hid": to})

    own_copy = pltpu.make_async_copy(tok_ref, tok.at[h], own_sem)
    own_copy.start()

    barrier = pltpu.get_barrier_semaphore()
    each(H - 1, lambda d: pl.semaphore_signal(
        barrier, inc=1, device_id={"hid": lax.rem(h + d + 1, H)}, device_id_type=MESH))
    each(X - 1, lambda d: pl.semaphore_signal(
        barrier, inc=1, device_id={"feat": x_peer(d + 1) * 2 + c}, device_id_type=MESH))
    pl.semaphore_signal(barrier, inc=1, device_id=pair, device_id_type=MESH)

    def start_gate_up(k):
        wg_copy(k).start()
        wu_copy(k).start()

    each(nch, start_gate_up)
    each(nd, lambda n: wd_copy(n).start())
    pl.semaphore_wait(barrier, H - 1 + X)

    each(H - 1, lambda d: tok_copy(d).start())
    own_copy.wait()
    each(H - 1, lambda d: tok_copy(d).wait_recv())

    def multiply(k):
        wg_copy(k).wait()
        wu_copy(k).wait()
        for j in range(rows // block):
            held = block // r_in
            lhs = tok[j * held:(j + 1) * held].reshape(block, tok.shape[2])
            for w, base in ((wg, 0), (wu, cn)):
                got = jnp.dot(lhs, w[k], preferred_element_type=F32).astype(BF16)
                got = got.reshape(ob // 2, 2, rf, cn)
                part[k, j * (ob // 2):(j + 1) * (ob // 2), :, :, base:base + cn] = got
        pair_copy(k).start()

    def across(k):
        pair_copy(k).wait_recv()

        def send(d):
            to = x_peer(d + 1)
            summed = part[k, to, c].astype(F32) + pair_in[k, to].astype(F32)
            x_out[k, d] = summed.astype(BF16)
            x_copy(k, d).start()

        each(X - 1, send)

    def activate(k):
        total = part[k, x, c].astype(F32) + pair_in[k, x].astype(F32)
        for d in range(X - 1):
            x_copy(k, d).wait_recv()
            total = total + x_in[k, d].astype(F32)
        gate, up = total[:, :cn], total[:, cn:]
        hid[k, f] = (gate / (1.0 + jnp.exp(-gate)) * up).astype(BF16)
        each(X - 1, lambda d: hx_copy(k, d).start())
        hp_copy(k).start()

    def forward(k):
        def step(d):
            hx_copy(k, d).wait_recv()
            hf_copy(k, d).start()

        each(X - 1, step)

    stages = (multiply, across, activate, forward)

    def turn(t, _):
        for lag, stage in enumerate(stages):
            k = t - lag

            @pl.when(jnp.logical_and(k >= 0, k < nch))
            def _():
                stage(k)

        return 0

    lax.fori_loop(0, nch + len(stages) - 1, turn, 0)

    def arrived(k):
        hp_copy(k).wait_recv()
        each(X - 1, lambda d: hf_copy(k, d).wait_recv())

    each(nch, arrived)

    def project(n, _):
        wd_copy(n).wait()
        for j in range(rows // block):
            first = j * ob
            lhs = jnp.concatenate(
                [hid[k, first:first + ob].reshape(block, cn) for k in range(nch)], axis=1)
            got = jnp.dot(lhs, wd[n], preferred_element_type=F32).astype(BF16)
            held = block // r_in
            o_part[n, j * held:(j + 1) * held] = got.reshape(held, r_in, dn)
        each(H - 1, lambda d: o_copy(n, d).start())
        return 0

    lax.fori_loop(0, nd, project, 0)

    for n in range(nd):
        each(H - 1, lambda d: o_copy(n, d).wait_recv())
        total = o_part[n, h].astype(F32)
        for d in range(H - 1):
            total = total + o_in[n, d].astype(F32)
        out_ref[:, n * dn:(n + 1) * dn] = total.astype(BF16)

    each(H - 1, lambda d: tok_copy(d).wait_send())

    def sent(k):
        pair_copy(k).wait_send()
        hp_copy(k).wait_send()

        def over(d):
            x_copy(k, d).wait_send()
            hx_copy(k, d).wait_send()
            hf_copy(k, d).wait_send()

        each(X - 1, over)

    each(nch, sent)
    each(nd, lambda n: each(H - 1, lambda d: o_copy(n, d).wait_send()))


def shards(H, F, tokens, gate_weight, up_weight, down_weight):
    r_in, k1 = tokens.shape
    n1 = gate_weight.shape[1]
    k2, n2 = down_weight.shape
    X = F // 2
    rf = r_in * H // F
    cn = min(512, n1)
    dn = min(256, n2)
    nch, nd = n1 // cn, n2 // dn
    dma = lambda *dims: pltpu.SemaphoreType.DMA(dims)
    buf = lambda *dims: pltpu.VMEM(dims, BF16)
    return pl.pallas_call(
        functools.partial(kernel, H, X),
        out_shape=jax.ShapeDtypeStruct((r_in, n2), BF16),
        in_specs=[pl.BlockSpec(memory_space=pl.ANY)] * 4,
        out_specs=pl.BlockSpec(memory_space=pltpu.VMEM),
        scratch_shapes=[
            buf(H, r_in, k1),
            buf(nch, k1, cn), buf(nch, k1, cn), buf(nd, k2, dn),
            buf(nch, X, 2, rf, 2 * cn), buf(nch, X, rf, 2 * cn),
            buf(nch, X - 1, rf, 2 * cn), buf(nch, X - 1, rf, 2 * cn),
            buf(nch, F, rf, cn),
            buf(nd, H, r_in, dn), buf(nd, H - 1, r_in, dn),
            dma(nch), dma(nch), dma(nd), pltpu.SemaphoreType.DMA,
            dma(H - 1), dma(H - 1),
            dma(nch), dma(nch), dma(nch, X - 1), dma(nch, X - 1),
            dma(nch), dma(nch), dma(nch, X - 1), dma(nch, X - 1),
            dma(nch, X - 1), dma(nch, X - 1),
            dma(nd, H - 1), dma(nd, H - 1),
        ],
        compiler_params=pltpu.CompilerParams(
            collective_id=0, has_side_effects=True, vmem_limit_bytes=60 * 2**20),
    )(tokens, gate_weight, up_weight, down_weight)


def solution(mesh):
    placed = (P(("grp", "hid"), "feat"), P("feat", "hid"), P("feat", "hid"), P("hid", "feat"))
    return jax.shard_map(
        functools.partial(shards, mesh.shape["hid"], mesh.shape["feat"]),
        mesh=mesh, in_specs=placed, out_specs=P(("grp", "hid"), "feat"), check_vma=False,
    )
```

time: 107 us -> 45.5 us (0.43)
  waiting for transfers between devices: 46.8 us -> 0 us
  Pallas kernels: 0 us -> 43.8 us
  blocking collectives: 22.7 us -> 0 us
  matrix products: 21.3 us -> 0 us
  between operations: 13.4 us -> 0.01 us
  other arithmetic: 2.11 us -> 0 us
  local copies, waits for them, and re-layouts: 0.01 us -> 1.47 us
    reduce_scatter x2 -> x0, waiting for transfers between devices: 46.7 us -> none  [the longest x1 26.5 us: shards(): lax.psum_scatter(jnp.concatenate([gate_part, up_part], axis=1).astype(jnp...]
    pallas_call x0 -> x1, Pallas kernels: none -> 43.8 us  [shards(): pl.pallas_call(functools.partial(kernel, H, X), out_shape=jax.ShapeDtypeS...]
    all_gather x2 -> x0, blocking collectives: 22.7 us -> none  [the longest x1 16 us: shards(): gathered = lax.all_gather(tokens, 'hid', axis=0, tiled=True)]
    dot_general x3 -> x0, matrix products: 21.3 us -> none  [the longest x1 9.49 us: shards(): jnp.dot(row_block, down_weight, preferred_element_type=jnp.float32)]
    unnamed x2 -> x1, local copies, waits for them, and re-layouts: 0.01 us -> 1.47 us
  transfers between devices with their start and end apart: 2 -> 0, of which waited for: 2 -> 0; matrix products, arithmetic and copies ran while one was open for 0% -> 0% of each run, Pallas kernels for 0% -> 0%
where the time goes in v1:
time: 45.5 us; the launch traced here: 45.3 us
  Pallas kernels  43.8 us (96%)
  local copies, waits for them, and re-layouts  1.47 us (3%)
    pallas_call x1, Pallas kernels, shards(): pl.pallas_call(functools.partial(kernel, H, X), out_shape=jax.ShapeDtypeS...  43.8 us
    unnamed x1, local copies, waits for them, and re-layouts  1.47 us

profile of v1, /device:TPU:0, one launch (start us, length us, event | category | flops | bytes accessed | tf_op | source)
XLA Modules:
  0.0 45.3 jit_solution(38423682110885851)
XLA Ops:
  0.0 43.8 %shard_map.46 = bf16[16,2048]{1,0:T(8,128)(2,1)} custom-call(bf16[16,2048]{1,0:T(8,128)(2,1)} %tok_ref.1, bf16[2048,4096]{1,0:T(8,128)(2,1)} %gate_ref.1, bf16[2048,4096]{1,0:T(8,128)(2,1)} %up_ref.1, bf16[4096,2048]{1,0:T(8,128)(2,1)} %down_ref.1), custom_call_target="tpu_custom_call" | custom-call | tf_op jit(solution)/shard_map/pallas_call | solution.py:221
  43.8 1.5 %copy.6 = bf16[16,2048]{1,0:T(8,128)(2,1)} copy(bf16[16,2048]{1,0:T(8,128)(2,1)} %shard_map.46) | data formatting | bytes 131072

commit v2 on v1

--- a/solution.py
+++ b/solution.py
@@ -149,10 +149,10 @@
 
         each(X - 1, step)
 
-    stages = (multiply, across, activate, forward)
+    stages = ((0, multiply), (1, across), (5, activate), (9, forward))
 
     def turn(t, _):
-        for lag, stage in enumerate(stages):
+        for lag, stage in stages:
             k = t - lag
 
             @pl.when(jnp.logical_and(k >= 0, k < nch))
@@ -161,7 +161,7 @@
 
         return 0
 
-    lax.fori_loop(0, nch + len(stages) - 1, turn, 0)
+    lax.fori_loop(0, nch + stages[-1][0], turn, 0)
 
     def arrived(k):
         hp_copy(k).wait_recv()
@@ -214,7 +214,7 @@
     X = F // 2
     rf = r_in * H // F
     cn = min(512, n1)
-    dn = min(256, n2)
+    dn = min(512, n2)
     nch, nd = n1 // cn, n2 // dn
     dma = lambda *dims: pltpu.SemaphoreType.DMA(dims)
     buf = lambda *dims: pltpu.VMEM(dims, BF16)

time: 45.5 us -> 38 us (0.84)
  Pallas kernels: 43.8 us -> 36.4 us
    pallas_call x1, Pallas kernels: 43.8 us -> 36.4 us  [shards(): pl.pallas_call(functools.partial(kernel, H, X), out_shape=jax.ShapeDtypeS...]
where the time goes in v2:
time: 38 us; the launch traced here: 37.9 us
  Pallas kernels  36.4 us (96%)
  local copies, waits for them, and re-layouts  1.47 us (4%)
    pallas_call x1, Pallas kernels, shards(): pl.pallas_call(functools.partial(kernel, H, X), out_shape=jax.ShapeDtypeS...  36.4 us
    unnamed x1, local copies, waits for them, and re-layouts  1.47 us

profile of v2, /device:TPU:0, one launch (start us, length us, event | category | flops | bytes accessed | tf_op | source)
XLA Modules:
  0.0 37.9 jit_solution(1464560918528192883)
XLA Ops:
  0.0 36.4 %shard_map.46 = bf16[16,2048]{1,0:T(8,128)(2,1)} custom-call(bf16[16,2048]{1,0:T(8,128)(2,1)} %tok_ref.1, bf16[2048,4096]{1,0:T(8,128)(2,1)} %gate_ref.1, bf16[2048,4096]{1,0:T(8,128)(2,1)} %up_ref.1, bf16[4096,2048]{1,0:T(8,128)(2,1)} %down_ref.1), custom_call_target="tpu_custom_call" | custom-call | tf_op jit(solution)/shard_map/pallas_call | solution.py:221
  36.4 1.5 %copy.6 = bf16[16,2048]{1,0:T(8,128)(2,1)} copy(bf16[16,2048]{1,0:T(8,128)(2,1)} %shard_map.46) | data formatting | bytes 131072

commit v3 on v2

--- a/solution.py
+++ b/solution.py
@@ -9,6 +9,7 @@
 
 MESH = pl.DeviceIdType.MESH
 F32, BF16 = jnp.float32, jnp.bfloat16
+X_LAG, H_LAG, D_LAG = 4, 7, 8
 
 
 def each(count, body):
@@ -21,12 +22,12 @@
 
 def kernel(
     H, X, tok_ref, gate_ref, up_ref, down_ref, out_ref,
-    tok, wg, wu, wd, part, pair_in, x_out, x_in, hid, o_part, o_in,
+    tok, wg, wu, wd, part, pair_in, x_out, x_in, hid, acc, o_part, o_in,
     wg_sem, wu_sem, wd_sem, own_sem, tok_s, tok_r, pair_s, pair_r, x_s, x_r,
     hp_s, hp_r, hx_s, hx_r, hf_s, hf_r, o_s, o_r,
 ):
     nch, _, cn = wg.shape
-    nd, _, dn = wd.shape
+    nd, _, _, dn = o_part.shape
     F = 2 * X
     rf = part.shape[3]
     r_in = tok.shape[1]
@@ -57,8 +58,9 @@
     def wu_copy(k):
         return pltpu.make_async_copy(cols(up_ref, k, cn), wu.at[k], wu_sem.at[k])
 
-    def wd_copy(n):
-        return pltpu.make_async_copy(cols(down_ref, n, dn), wd.at[n], wd_sem.at[n])
+    def wd_copy(k):
+        rows_k = pl.ds(pl.multiple_of(k * cn, cn), cn)
+        return pltpu.make_async_copy(down_ref.at[rows_k], wd.at[k], wd_sem.at[k])
 
     def tok_copy(d):
         to = lax.rem(h + d + 1, H)
@@ -102,7 +104,8 @@
         wu_copy(k).start()
 
     each(nch, start_gate_up)
-    each(nd, lambda n: wd_copy(n).start())
+    each(nch, lambda k: wd_copy(k).start())
+    acc[...] = jnp.zeros_like(acc)
     pl.semaphore_wait(barrier, H - 1 + X)
 
     each(H - 1, lambda d: tok_copy(d).start())
@@ -149,39 +152,46 @@
 
         each(X - 1, step)
 
-    stages = ((0, multiply), (1, across), (5, activate), (9, forward))
-
-    def turn(t, _):
-        for lag, stage in stages:
-            k = t - lag
-
-            @pl.when(jnp.logical_and(k >= 0, k < nch))
-            def _():
-                stage(k)
-
-        return 0
-
-    lax.fori_loop(0, nch + stages[-1][0], turn, 0)
-
     def arrived(k):
         hp_copy(k).wait_recv()
         each(X - 1, lambda d: hf_copy(k, d).wait_recv())
-
-    each(nch, arrived)
-
-    def project(n, _):
-        wd_copy(n).wait()
+        wd_copy(k).wait()
+
+    def product(k, j, n):
+        lhs = hid[k, j * ob:(j + 1) * ob].reshape(block, cn)
+        got = jnp.dot(lhs, wd[k, :, n * dn:(n + 1) * dn], preferred_element_type=F32)
+        return acc[j * block:(j + 1) * block, n * dn:(n + 1) * dn] + got
+
+    def accumulate(k):
+        arrived(k)
         for j in range(rows // block):
-            first = j * ob
-            lhs = jnp.concatenate(
-                [hid[k, first:first + ob].reshape(block, cn) for k in range(nch)], axis=1)
-            got = jnp.dot(lhs, wd[n], preferred_element_type=F32).astype(BF16)
-            held = block // r_in
+            for n in range(nd):
+                acc[j * block:(j + 1) * block, n * dn:(n + 1) * dn] = product(k, j, n)
+
+    stages = (
+        (0, nch, multiply), (1, nch, across), (X_LAG, nch, activate),
+        (H_LAG, nch, forward), (D_LAG, nch - 1, accumulate),
+    )
+
+    def turn(t, _):
+        for lag, count, stage in stages:
+            k = t - lag
+
+            @pl.when(jnp.logical_and(k >= 0, k < count))
+            def _():
+                stage(k)
+
+        return 0
+
+    lax.fori_loop(0, max(lag + count for lag, count, _ in stages), turn, 0)
+
+    arrived(nch - 1)
+    held = block // r_in
+    for n in range(nd):
+        for j in range(rows // block):
+            got = product(nch - 1, j, n).astype(BF16)
             o_part[n, j * held:(j + 1) * held] = got.reshape(held, r_in, dn)
         each(H - 1, lambda d: o_copy(n, d).start())
-        return 0
-
-    lax.fori_loop(0, nd, project, 0)
 
     for n in range(nd):
         each(H - 1, lambda d: o_copy(n, d).wait_recv())
@@ -214,7 +224,7 @@
     X = F // 2
     rf = r_in * H // F
     cn = min(512, n1)
-    dn = min(512, n2)
+    dn = min(2048, n2)
     nch, nd = n1 // cn, n2 // dn
     dma = lambda *dims: pltpu.SemaphoreType.DMA(dims)
     buf = lambda *dims: pltpu.VMEM(dims, BF16)
@@ -225,12 +235,13 @@
         out_specs=pl.BlockSpec(memory_space=pltpu.VMEM),
         scratch_shapes=[
             buf(H, r_in, k1),
-            buf(nch, k1, cn), buf(nch, k1, cn), buf(nd, k2, dn),
+            buf(nch, k1, cn), buf(nch, k1, cn), buf(nch, cn, n2),
             buf(nch, X, 2, rf, 2 * cn), buf(nch, X, rf, 2 * cn),
             buf(nch, X - 1, rf, 2 * cn), buf(nch, X - 1, rf, 2 * cn),
             buf(nch, F, rf, cn),
+            pltpu.VMEM((r_in * H, n2), F32),
             buf(nd, H, r_in, dn), buf(nd, H - 1, r_in, dn),
-            dma(nch), dma(nch), dma(nd), pltpu.SemaphoreType.DMA,
+            dma(nch), dma(nch), dma(nch), pltpu.SemaphoreType.DMA,
             dma(H - 1), dma(H - 1),
             dma(nch), dma(nch), dma(nch, X - 1), dma(nch, X - 1),
             dma(nch), dma(nch), dma(nch, X - 1), dma(nch, X - 1),

time: 38 us -> 37.2 us (0.979)
  Pallas kernels: 36.4 us -> 35.6 us
    pallas_call x1, Pallas kernels: 36.4 us -> 35.6 us  [shards(): pl.pallas_call(functools.partial(kernel, H, X), out_shape=jax.ShapeDtypeS...]
where the time goes in v3:
time: 37.2 us; the launch traced here: 37.1 us
  Pallas kernels  35.6 us (96%)
  local copies, waits for them, and re-layouts  1.47 us (4%)
    pallas_call x1, Pallas kernels, shards(): pl.pallas_call(functools.partial(kernel, H, X), out_shape=jax.ShapeDtypeS...  35.6 us
    unnamed x1, local copies, waits for them, and re-layouts  1.47 us

profile of v3, /device:TPU:0, one launch (start us, length us, event | category | flops | bytes accessed | tf_op | source)
XLA Modules:
  0.0 37.1 jit_solution(2635113453196725994)
XLA Ops:
  0.0 35.6 %shard_map.46 = bf16[16,2048]{1,0:T(8,128)(2,1)} custom-call(bf16[16,2048]{1,0:T(8,128)(2,1)} %tok_ref.1, bf16[2048,4096]{1,0:T(8,128)(2,1)} %gate_ref.1, bf16[2048,4096]{1,0:T(8,128)(2,1)} %up_ref.1, bf16[4096,2048]{1,0:T(8,128)(2,1)} %down_ref.1), custom_call_target="tpu_custom_call" | custom-call | tf_op jit(solution)/shard_map/pallas_call | solution.py:231
  35.6 1.5 %copy.6 = bf16[16,2048]{1,0:T(8,128)(2,1)} copy(bf16[16,2048]{1,0:T(8,128)(2,1)} %shard_map.46) | data formatting | bytes 131072

commit v4 on v3

--- a/solution.py
+++ b/solution.py
@@ -9,7 +9,7 @@
 
 MESH = pl.DeviceIdType.MESH
 F32, BF16 = jnp.float32, jnp.bfloat16
-X_LAG, H_LAG, D_LAG = 4, 7, 8
+X_LAG, H_LAG, D_LAG = 4, 6, 7
 
 
 def each(count, body):

time: 37.2 us -> 38.9 us (1.046)
  Pallas kernels: 35.6 us -> 37.2 us
    pallas_call x1, Pallas kernels: 35.6 us -> 37.2 us  [shards(): pl.pallas_call(functools.partial(kernel, H, X), out_shape=jax.ShapeDtypeS...]
where the time goes in v4:
time: 38.9 us; the launch traced here: 38.7 us
  Pallas kernels  37.2 us (96%)
  local copies, waits for them, and re-layouts  1.47 us (4%)
    pallas_call x1, Pallas kernels, shards(): pl.pallas_call(functools.partial(kernel, H, X), out_shape=jax.ShapeDtypeS...  37.2 us
    unnamed x1, local copies, waits for them, and re-layouts  1.47 us

profile of v4, /device:TPU:0, one launch (start us, length us, event | category | flops | bytes accessed | tf_op | source)
XLA Modules:
  0.0 38.7 jit_solution(13877879281233616774)
XLA Ops:
  0.0 37.2 %shard_map.46 = bf16[16,2048]{1,0:T(8,128)(2,1)} custom-call(bf16[16,2048]{1,0:T(8,128)(2,1)} %tok_ref.1, bf16[2048,4096]{1,0:T(8,128)(2,1)} %gate_ref.1, bf16[2048,4096]{1,0:T(8,128)(2,1)} %up_ref.1, bf16[4096,2048]{1,0:T(8,128)(2,1)} %down_ref.1), custom_call_target="tpu_custom_call" | custom-call | tf_op jit(solution)/shard_map/pallas_call | solution.py:231
  37.2 1.5 %copy.6 = bf16[16,2048]{1,0:T(8,128)(2,1)} copy(bf16[16,2048]{1,0:T(8,128)(2,1)} %shard_map.46) | data formatting | bytes 131072
